TPU v7x, 32 devices: a whole 2x2x4 slice. The times are simulated.
32 devices in a mesh: sph: 8 (over y, x, core), grp: 4 (over z).
Axes of the slice: x: 2, y: 2, z: 4, core: 2. Of those that a mesh axis runs over, the one named last changes fastest.
Arguments:
- pixel_features: bfloat16 [32768, 512], P(('sph', 'grp')), may hold values from -6 to 6
- tier_one_codes: bfloat16 [2048, 512], P(('sph', 'grp')), may hold values from -6 to 6
- tier_two_codes: bfloat16 [128, 512], P(('sph', 'grp')), may hold values from -6 to 6
- tier_three_codes: bfloat16 [8, 512], P('sph'), may hold values from -6 to 6
- tier_one_picks: int32 [2048, 16], P(('sph', 'grp')), may hold values from 0 to 2047, as said below
- tier_two_picks: int32 [2048, 16], P(('sph', 'grp')), may hold values from 0 to 127, as said below
- tier_three_picks: int32 [2048, 16], P(('sph', 'grp')), may hold values from 0 to 7, as said below
- probe_matrix: bfloat16 [3, 512, 512], replicated, may hold values from -0.25 to 0.25
- address_matrix: bfloat16 [3, 512, 512], replicated, may hold values from -0.25 to 0.25
- content_matrix: bfloat16 [3, 512, 512], replicated, may hold values from -0.25 to 0.25
- merge_matrix: bfloat16 [3, 512, 512], replicated, may hold values from -0.25 to 0.25
- expand_matrix: bfloat16 [3, 512, 1024], replicated, may hold values from -0.25 to 0.25
- shrink_matrix: bfloat16 [3, 1024, 512], replicated, may hold values from -0.1875 to 0.1875
- rescale_factors: float32 [3, 3, 512], replicated, may hold values from 0.25 to 1.75
- logit_scaling: float32 [3, 8], replicated, may hold values from 0.5 to 2
Outputs:
- encoded: bfloat16 [32768, 512], P(('sph', 'grp'))
Inputs may be any that keep to these rules, and one draw needn't show every extreme that they name: `tier_one_picks`: entry 0 of block b's list is b, its own level-one parent; every entry lies within 64 of b. `tier_two_picks`: entry 0 of block b's list is b // 16, its level-two parent; every entry lies in the same aligned run of 16 level-two latents as entry 0. `tier_three_picks`: entry 0 of block b's list is b // 256, its level-three parent.
All inputs are finite; a program needn't handle non-finite values.
Results may differ from a plain program's by a relative error of at most 0.01.
Values may be sent and summed in bfloat16 or wider, within the bound.
A program may use at most 128 MiB of HBM per device.

v0:
```python
import math

import jax
import jax.numpy as jnp
from jax import lax
from jax.sharding import PartitionSpec as P

eps = 1e-06


def with_halo(block, sides, width):
    for axis, dim in sides:
        count = lax.axis_size(axis)
        forward = [(i, i + 1) for i in range(count - 1)]
        backward = [(target, source) for source, target in forward]
        low = lax.ppermute(
            lax.slice_in_dim(block, block.shape[dim] - width, None, axis=dim), axis, forward
        )
        high = lax.ppermute(lax.slice_in_dim(block, 0, width, axis=dim), axis, backward)
        block = jnp.concatenate([low, block, high], axis=dim)
    return block


def normalize(values_in, gain_vec):
    return (
        values_in
        * lax.rsqrt(jnp.mean(values_in * values_in, axis=-1, keepdims=True) + eps)
        * gain_vec
    )


def per_head(values_in, channel_groups):
    dims_shape = values_in.shape
    grouped = values_in.reshape(
        dims_shape[:-1] + (channel_groups, dims_shape[-1] // channel_groups)
    )
    grouped = grouped * lax.rsqrt(jnp.mean(grouped * grouped, axis=-1, keepdims=True) + eps)
    return grouped.reshape(dims_shape)


def refresh(latent, tier_ordinal, expand_matrix, shrink_matrix, rescale_factors):
    running_features = latent.astype(jnp.float32)
    mlp_in = normalize(running_features, rescale_factors[tier_ordinal, 1]).astype(jnp.bfloat16)
    hidden = jax.nn.silu(
        jnp.dot(mlp_in, expand_matrix[tier_ordinal], preferred_element_type=jnp.float32)
    ).astype(jnp.bfloat16)
    renewed = (
        running_features
        + jnp.dot(hidden, shrink_matrix[tier_ordinal], preferred_element_type=jnp.float32)
    ).astype(jnp.bfloat16)
    return lax.optimization_barrier(renewed)


def project(renewed, tier_ordinal, address_matrix, content_matrix, rescale_factors, channel_groups):
    kv_in = normalize(renewed.astype(jnp.float32), rescale_factors[tier_ordinal, 2]).astype(
        jnp.bfloat16
    )
    key_part = per_head(
        jnp.dot(kv_in, address_matrix[tier_ordinal], preferred_element_type=jnp.float32),
        channel_groups,
    ).astype(jnp.bfloat16)
    value_part = jnp.dot(
        kv_in, content_matrix[tier_ordinal], preferred_element_type=jnp.float32
    ).astype(jnp.bfloat16)
    return jnp.concatenate([key_part, value_part], axis=1)


def mix_across_tiers(
    running_features,
    gather_entries,
    tier_positions,
    tier_ordinal,
    probe_matrix,
    merge_matrix,
    rescale_factors,
    logit_scaling,
):
    row_count, feature = running_features.shape
    blocks = tier_positions.shape[0]
    channel_groups = logit_scaling.shape[1]
    group_dimension = feature // channel_groups
    table_rows = gather_entries.shape[0]
    normed = normalize(running_features, rescale_factors[tier_ordinal, 0]).astype(jnp.bfloat16)
    probe_heads = probe_matrix[tier_ordinal].reshape(feature, channel_groups, group_dimension)
    queries = jnp.einsum("rc,chd->hrd", normed, probe_heads, preferred_element_type=jnp.float32)
    queries = queries * lax.rsqrt(jnp.mean(queries * queries, axis=-1, keepdims=True) + eps)
    queries = queries.astype(jnp.bfloat16).reshape(
        channel_groups, blocks, row_count // blocks, group_dimension
    )
    key_heads = jnp.transpose(
        gather_entries[:, :feature].reshape(table_rows, channel_groups, group_dimension), (1, 0, 2)
    )
    value_heads = jnp.transpose(
        gather_entries[:, feature:].reshape(table_rows, channel_groups, group_dimension), (1, 0, 2)
    )
    key_picked = jnp.take(key_heads, tier_positions, axis=1)
    value_picked = jnp.take(value_heads, tier_positions, axis=1)
    affinity_logits = jnp.einsum(
        "hbid,hbjd->hbij", queries, key_picked, preferred_element_type=jnp.float32
    )
    affinity_logits = (
        affinity_logits
        * (logit_scaling[tier_ordinal] / math.sqrt(group_dimension))[:, None, None, None]
    )
    weights = jnp.exp(affinity_logits)
    weights = (weights / jnp.sum(weights, axis=-1, keepdims=True)).astype(jnp.bfloat16)
    mixture = jnp.einsum(
        "hbij,hbjd->hbid", weights, value_picked, preferred_element_type=jnp.float32
    )
    mixture = mixture.astype(jnp.bfloat16).reshape(channel_groups, row_count, group_dimension)
    merge_heads = merge_matrix[tier_ordinal].reshape(channel_groups, group_dimension, feature)
    return running_features + jnp.einsum(
        "hrd,hde->re", mixture, merge_heads, preferred_element_type=jnp.float32
    )


def per_device(
    pixel_features,
    tier_one_codes,
    tier_two_codes,
    tier_three_codes,
    tier_one_picks,
    tier_two_picks,
    tier_three_picks,
    probe_matrix,
    address_matrix,
    content_matrix,
    merge_matrix,
    expand_matrix,
    shrink_matrix,
    rescale_factors,
    logit_scaling,
):
    channel_groups = logit_scaling.shape[1]
    block_count = tier_one_codes.shape[0]
    device_index = lax.axis_index(("sph", "grp"))
    sphere_index = lax.axis_index("sph")
    renewed_one = refresh(tier_one_codes, 0, expand_matrix, shrink_matrix, rescale_factors)
    renewed_two = refresh(tier_two_codes, 1, expand_matrix, shrink_matrix, rescale_factors)
    renewed_three = refresh(tier_three_codes, 2, expand_matrix, shrink_matrix, rescale_factors)
    first_table = with_halo(
        project(renewed_one, 0, address_matrix, content_matrix, rescale_factors, channel_groups),
        ((("sph", "grp"), 0),),
        block_count,
    )
    second_table = lax.all_gather(
        project(renewed_two, 1, address_matrix, content_matrix, rescale_factors, channel_groups),
        "grp",
        axis=0,
        tiled=True,
    )
    third_table = lax.all_gather(
        project(renewed_three, 2, address_matrix, content_matrix, rescale_factors, channel_groups),
        "sph",
        axis=0,
        tiled=True,
    )
    local_first = tier_one_picks - (device_index * block_count - block_count)
    local_second = tier_two_picks - sphere_index * second_table.shape[0]
    running_features = pixel_features.astype(jnp.float32)
    running_features = mix_across_tiers(
        running_features,
        first_table,
        local_first,
        0,
        probe_matrix,
        merge_matrix,
        rescale_factors,
        logit_scaling,
    )
    running_features = mix_across_tiers(
        running_features,
        second_table,
        local_second,
        1,
        probe_matrix,
        merge_matrix,
        rescale_factors,
        logit_scaling,
    )
    running_features = mix_across_tiers(
        running_features,
        third_table,
        tier_three_picks,
        2,
        probe_matrix,
        merge_matrix,
        rescale_factors,
        logit_scaling,
    )
    return running_features.astype(jnp.bfloat16)


def solution(mesh):
    placed = (
        P(("sph", "grp"), None),
        P(("sph", "grp"), None),
        P(("sph", "grp"), None),
        P("sph", None),
        P(("sph", "grp"), None),
        P(("sph", "grp"), None),
        P(("sph", "grp"), None),
        P(),
        P(),
        P(),
        P(),
        P(),
        P(),
        P(),
        P(),
    )
    return jax.shard_map(
        per_device, mesh=mesh, in_specs=placed, out_specs=P(("sph", "grp"), None), check_vma=False
    )
```

profile of v0, /device:TPU:0, one launch (start us, length us, event | category | flops | bytes accessed | tf_op | source)
XLA Modules:
  0.0 146.6 jit_solution(8718872279876294952)
XLA Ops:
  0.0 1.5 %fusion.149 = (f32[1,1,512]{2,1,0:T(1,128)}, f32[1,1,512]{2,1,0:T(1,128)}, f32[1,1,512]{2,1,0:T(1,128)}, f32[1,1,512]{2,1,0:T(1,128)}, f32[1,1,512]{2,1,0:T(1,12...) fusion(f32[3,3,512]{2,1,0:T(4,128)} %param.34), kind=kLoop, calls=%fused_computation.208 | loop fusion | bytes 28672 | tf_op jit(solution)/shard_map/slice | solution.py:83
  1.5 1.0 fusion.90
  2.5 2.1 %fusion.35 = bf16[64,512]{1,0:T(8,128)(2,1)S(1)} fusion(bf16[3,1024,512]{2,1,0:T(8,128)(2,1)} %param.33, bf16[3,512,1024]{2,1,0:T(8,128)(2,1)} %param.32, bf16[64,512]{1,0:T(8,128)(2,1)} %param.22, f32[512]{0:T(512)S(1)} %bitcast.253, f32[64]{0:T(128)S(1)} %add_rsqrt_fusion.12), kind=kOutput, calls=%fused_computation.63 | convolution fusion | flops 134774784 | bytes 2296064 | tf_op jit(solution)/shard_map/dot_general | solution.py:49
  4.7 0.9 slice_bitcast_fusion
  6.3 1.3 convolution_convert_fusion
  7.7 4.9 %collective-permute-start = (bf16[64,1024]{1,0:T(8,128)(2,1)S(1)}, bf16[64,1024]{1,0:T(8,128)(2,1)S(1)}, u32[]{:S(2)}, u32[]{:S(2)}) collective-permute-start(bf16[64,1024]{1,0:T(8,128)(2,1)S(1)} %pad_maximum_fusion.1), channel_id=1, source_target_pairs={{0,1},{1,2},{2,3},{3,4},{4,5},{5,6},{6,7},{7,8},{8,9},{9,10},{10,1... | collective-permute-start | bytes 393224 | tf_op jit(solution)/shard_map/ppermute | solution.py:16
  12.6 1.3 collective-permute-start.1
  13.9 0.6 multiply_reduce_fusion.8
  15.2 1.5 %fusion.43 = f32[1,1024]{1,0:T(1,128)S(1)} fusion(bf16[3,512,1024]{2,1,0:T(8,128)(2,1)} %param.32, f32[3,3,512]{2,1,0:T(4,128)S(1)} %copy-done.11, bf16[1,512]{1,0:T(2,128)(2,1)S(1)} %copy-done.14, f32[]{:T(128)S(6)} %rsqrt.124), kind=kOutput, calls=%fused_computation.74 | convolution fusion | flops 1050624 | bytes 1056772 | tf_op jit(solution)/shard_map/dot_general | solution.py:45
  16.7 1.5 %fusion.37 = bf16[1,512]{1,0:T(2,128)(2,1)S(1)} fusion(bf16[1024,1]{0,1:T(2,128)(2,1)S(1)} %reshape.381, bf16[3,1024,512]{2,1,0:T(8,128)(2,1)} %param.33, bf16[1,512]{1,0:T(2,128)(2,1)S(1)} %copy-done.14), kind=kOutput, calls=%fused_computation.69 | convolution fusion | flops 1050112 | bytes 1052672 | tf_op jit(solution)/shard_map/dot_general | solution.py:49
  18.2 0.6 multiply_reduce_fusion.7
  19.7 1.8 %fusion.70 = f32[1,512]{1,0:T(1,128)} fusion(bf16[3,512,512]{2,1,0:T(8,128)(2,1)} %param.30, f32[3,3,512]{2,1,0:T(4,128)S(1)} %copy-done.11, bf16[1,512]{1,0:T(2,128)(2,1)S(1)} %fusion.37, f32[]{:T(128)S(6)} %rsqrt.125), kind=kOutput, calls=%fused_computation.101 | convolution fusion | flops 526336 | bytes 530436 | tf_op jit(solution)/shard_map/dot_general | solution.py:62
  21.5 0.6 compare_select_fusion
  22.1 0.6 compare_and_fusion
  23.0 1.5 %copy.175 = bf16[1024,512]{0,1:T(8,128)(2,1)S(1)} copy(bf16[1024,512]{1,0:T(8,128)(2,1)} %param.21) | data formatting | bytes 2097152 | tf_op args[0]
  24.7 2.0 %multiply_reduce_fusion.4 = (f32[8,1024]{1,0:T(8,128)S(1)}, f32[1024,512]{0,1:S(1)}) fusion(bf16[1024,512]{0,1:T(8,128)(2,1)S(1)} %copy.175, f32[512]{0:T(512)S(1)} %bitcast.252, f32[1024]{0:T(1024)S(1)} %add_rsqrt_fusion.7, bf16[3,512,512]{2,1,0:T(8,128)(2,1)} %param.28), kind=kOutput, calls=%fused_computation.54 | convolution fusion | flops 540008448 | bytes 3708928
  27.0 1.1 copy.178
  28.1 2.7 %fusion.146 = (bf16[1,512,512]{2,1,0:T(8,128)(2,1)}, bf16[1,512,512]{2,1,0:T(8,128)(2,1)}, bf16[1,512,512]{2,1,0:T(8,128)(2,1)}) fusion(bf16[3,512,512]{2,1,0:T(8,128)(2,1)} %param.31), kind=kLoop, calls=%fused_computation.205 | loop fusion | bytes 3145728 | tf_op jit(solution)/shard_map/slice | solution.py:111
  30.9 2.0 %fusion.36 = bf16[4,512]{1,0:T(4,128)(2,1)S(1)} fusion(bf16[3,1024,512]{2,1,0:T(8,128)(2,1)} %param.33, bf16[3,512,1024]{2,1,0:T(8,128)(2,1)} %param.32, bf16[4,512]{1,0:T(4,128)(2,1)S(1)} %copy-done.23, f32[512]{0:T(512)S(1)} %bitcast.251, f32[4]{0:T(128)S(1)} %add_rsqrt_fusion.10), kind=kOutput, calls=%fused_computation.66 | convolution fusion | flops 8423424 | bytes 2112000 | tf_op jit(solution)/shard_map/dot_general | solution.py:49
  33.8 1.3 convolution_convert_fusion.1
  35.1 1.1 multiply_reduce_fusion.6
  36.4 14.4 %all-gather = bf16[4,4,1024]{2,1,0:T(4,128)(2,1)S(1)} all-gather(bf16[1,4,1024]{2,1,0:T(4,128)(2,1)S(1)} %maximum_bitcast_fusion), channel_id=1, replica_groups=mesh['sph'=8,'grp'=4] {'grp'}, dimensions={0}, use_global_device_ids=true | all-gather | bytes 40960 | tf_op jit(solution)/shard_map/all_gather | solution.py:146
  50.9 0.7 compare_and_fusion.1
  51.8 0.7 copy.196
  52.6 7.6 %gather_fusion.2 = bf16[1024,8,64]{2,1,0:T(8,128)(2,1)} fusion(bf16[8,16,64]{2,0,1:T(8,128)(2,1)S(1)} %bitcast.218, s32[1024]{0:T(1024)S(1)} %broadcast_clamp_fusion.1), kind=kCustom, calls=%fused_computation.1.clone | custom fusion | bytes 2101248 | tf_op jit(solution)/shard_map/jit(_take)/gather | solution.py:96
  60.2 7.6 %gather_fusion.3 = bf16[1024,8,64]{2,1,0:T(8,128)(2,1)} fusion(bf16[8,16,64]{2,0,1:T(8,128)(2,1)S(1)} %bitcast.219, s32[1024]{0:T(1024)S(1)} %broadcast_clamp_fusion.1), kind=kCustom, calls=%fused_computation.4.clone | custom fusion | bytes 2101248 | tf_op jit(solution)/shard_map/jit(_take)/gather | solution.py:97
  68.2 12.2 %all-gather.1 = bf16[8,1,1024]{2,1,0:T(2,128)(2,1)S(1)} all-gather(bf16[1,1,1024]{2,1,0:T(2,128)(2,1)S(1)} %maximum_bitcast_fusion.1), channel_id=1, replica_groups=mesh['sph'=8,'grp'=4] {'sph'}, dimensions={0}, use_global_device_ids=true | all-gather | bytes 18432 | tf_op jit(solution)/shard_map/all_gather | solution.py:152
  80.7 0.7 copy.209
  81.5 7.8 %gather_fusion.4 = bf16[1024,8,64]{2,1,0:T(8,128)(2,1)} fusion(bf16[8,8,64]{2,0,1:T(8,128)(2,1)S(1)} %bitcast.216, s32[1024]{0:T(1024)S(1)} %broadcast_clamp_fusion), kind=kCustom, calls=%fused_computation.2.clone | custom fusion | bytes 2101248 | tf_op jit(solution)/shard_map/jit(_take)/gather | solution.py:96
  89.2 7.6 %gather_fusion.5 = bf16[1024,8,64]{2,1,0:T(8,128)(2,1)} fusion(bf16[8,8,64]{2,0,1:T(8,128)(2,1)S(1)} %bitcast.217, s32[1024]{0:T(1024)S(1)} %broadcast_clamp_fusion), kind=kCustom, calls=%fused_computation.5.clone | custom fusion | bytes 2101248 | tf_op jit(solution)/shard_map/jit(_take)/gather | solution.py:97
  97.4 0.9 pad_maximum_fusion
  99.1 7.6 %gather_fusion.1 = bf16[1024,8,64]{2,1,0:T(8,128)(2,1)} fusion(bf16[8,192,64]{2,0,1:T(8,128)(2,1)S(1)} %bitcast.220, s32[1024]{0:T(1024)S(1)} %broadcast_clamp_fusion.2), kind=kCustom, calls=%fused_computation.3.clone | custom fusion | bytes 2101248 | tf_op jit(solution)/shard_map/jit(_take)/gather | solution.py:97
  106.7 7.6 %gather_fusion = bf16[1024,8,64]{2,1,0:T(8,128)(2,1)} fusion(bf16[8,192,64]{2,0,1:T(8,128)(2,1)S(1)} %bitcast.221, s32[1024]{0:T(1024)S(1)} %broadcast_clamp_fusion.2), kind=kCustom, calls=%fused_computation.clone | custom fusion | bytes 2101248 | tf_op jit(solution)/shard_map/jit(_take)/gather | solution.py:96
  114.4 3.5 %select_bitcast_fusion.1 = (bf16[8,64,16,64]{3,0,2,1:T(8,128)(2,1)S(1)}, bf16[8,64,16,64]{3,0,2,1:T(8,128)(2,1)S(1)}) fusion(bf16[64,16,8,64]{3,2,1,0:T(8,128)(2,1)} %bitcast.224, pred[64,16]{1,0:T(8,128)(4,1)S(1)} %copy.179, bf16[64,16,8,64]{3,2,1,0:T(8,128)(2,1)} %bitcast.223), kind=kLoop, calls=%fused_computation.41 | loop fusion | flops 1048576 | bytes 4195328 | tf_op jit(solution)/shard_map/jit(_take)/select_n | solution.py:96
  117.9 1.4 fusion
  119.4 1.6 %fusion.26 = bf16[8,64,16,64]{3,2,1,0:T(8,128)(2,1)S(1)} fusion(bf16[8,64,16,64]{3,0,2,1:T(8,128)(2,1)S(1)} %get-tuple-element.31, f32[8,64,16,16]{2,3,1,0:T(8,128)S(1)} %get-tuple-element.40, f32[8,64,16]{2,1,0:T(8,128)S(1)} %get-tuple-element.39, f32[8]{0:T(128)S(1)} %get-tuple-element.33), kind=kOutput, calls=%fused_computation.59 | convolution fusion | flops 17694720 | bytes 2654240 | tf_op jit(solution)/shard_map/hbij,hbjd->hbid/dot_general | solution.py:107
  121.1 1.3 multiply_reduce_fusion.3
  122.4 2.3 %multiply_reduce_fusion.2 = (f32[8,1024]{1,0:T(8,128)S(1)}, f32[1024,512]{0,1:S(1)}) fusion(f32[1024,512]{0,1:T(8,128)S(1)} %get-tuple-element.44, f32[512]{0:T(512)S(1)} %bitcast.245, f32[1024]{0:T(1024)S(1)} %add_rsqrt_fusion.5, bf16[3,512,512]{2,1,0:T(8,128)(2,1)} %param.28), kind=kOutput, calls=%fused_computation.49 | convolution fusion | flops 539484160 | bytes 4757504
  125.0 1.1 copy.195
  126.1 4.3 %fusion.1 = (f32[8,64,16]{2,1,0:T(8,128)S(1)}, f32[8,64,16,16]{2,3,1,0:T(8,128)S(1)}) fusion(f32[8]{0:T(128)S(1)} %copy-done.27, bf16[8,64,16,64]{3,2,1,0:T(8,128)(2,1)S(1)} %bitcast.226, bf16[64,16,8,64]{3,2,1,0:T(8,128)(2,1)} %bitcast.229, pred[64,16]{1,0:T(8,128)(4,1)S(1)} %copy-done.21), kind=kOutput, calls=%fused_computation.13 | convolution fusion | flops 17555456 | bytes 2655264 | tf_op jit(solution)/shard_map/hbid,hbjd->hbij/dot_general | solution.py:98
  130.5 2.1 %fusion.29 = bf16[8,64,16,64]{3,2,1,0:T(8,128)(2,1)S(1)} fusion(bf16[64,16,8,64]{3,2,1,0:T(8,128)(2,1)S(1)} %bitcast.228, pred[64,16]{1,0:T(8,128)(4,1)S(1)} %copy-done.21, f32[8,64,16,16]{2,3,1,0:T(8,128)S(1)} %get-tuple-element.48, f32[8,64,16]{2,1,0:T(8,128)S(1)} %get-tuple-element.47, f32[8]{0:T(128)S(1)} %copy-done.27), kind=kOutput, calls=%fused_computation.60 | convolution fusion | flops 18219008 | bytes 2655264 | tf_op jit(solution)/shard_map/hbij,hbjd->hbid/dot_general | solution.py:107
  132.6 1.3 multiply_reduce_fusion.1
  134.0 1.9 %multiply_reduce_fusion = (f32[8,1024]{1,0:T(8,128)S(1)}, f32[1024,512]{0,1:S(1)}) fusion(f32[1024,512]{0,1:T(8,128)S(1)} %get-tuple-element.50, f32[512]{0:T(512)S(1)} %bitcast.244, f32[1024]{0:T(1024)S(1)} %add_rsqrt_fusion.3, bf16[3,512,512]{2,1,0:T(8,128)(2,1)} %param.28), kind=kOutput, calls=%fused_computation.44 | convolution fusion | flops 539484160 | bytes 4757504
  136.1 1.8 %copy.208 = bf16[8,1024,64]{2,1,0:T(8,128)(2,1)} copy(bf16[8,1024,64]{1,2,0:T(8,128)(2,1)S(1)} %multiply_convert_fusion) | data formatting | bytes 2097152 | tf_op jit(solution)/shard_map/convert_element_type | solution.py:87
  138.0 3.9 %fusion.2 = (f32[8,64,16]{2,1,0:T(8,128)S(1)}, f32[8,64,16,16]{2,3,1,0:T(8,128)S(1)}) fusion(f32[8]{0:T(128)S(1)} %copy-done.26, bf16[8,64,16,64]{3,2,1,0:T(8,128)(2,1)} %bitcast.225, bf16[64,16,8,64]{3,2,1,0:T(8,128)(2,1)} %bitcast.231, pred[64,16]{1,0:T(8,128)(4,1)S(1)} %copy-done.22), kind=kOutput, calls=%fused_computation.14 | convolution fusion | flops 17555456 | bytes 2655264 | tf_op jit(solution)/shard_map/hbid,hbjd->hbij/dot_general | solution.py:98
  141.9 2.1 %fusion.32 = bf16[8,64,16,64]{3,2,1,0:T(8,128)(2,1)S(1)} fusion(bf16[64,16,8,64]{3,2,1,0:T(8,128)(2,1)S(1)} %bitcast.230, pred[64,16]{1,0:T(8,128)(4,1)S(1)} %copy-done.22, f32[8,64,16,16]{2,3,1,0:T(8,128)S(1)} %get-tuple-element.54, f32[8,64,16]{2,1,0:T(8,128)S(1)} %get-tuple-element.53, f32[8]{0:T(128)S(1)} %copy-done.26), kind=kOutput, calls=%fused_computation.61 | convolution fusion | flops 18219008 | bytes 2655264 | tf_op jit(solution)/shard_map/hbij,hbjd->hbid/dot_general | solution.py:107
  144.0 1.3 fusion.6
  145.3 1.3 copy.218
  (126 shorter events, 6.2 us)
Async XLA Ops:
  0.0 4.7 %copy-start.7 = (bf16[3,512,512]{2,1,0:T(8,128)(2,1)S(1)}, bf16[3,512,512]{2,1,0:T(8,128)(2,1)}, u32[]{:S(2)}) copy-start(bf16[3,512,512]{2,1,0:T(8,128)(2,1)} %param.29) | copy-start | bytes 4718596
  5.6 8.3 %copy-start.14 = (bf16[1,512]{1,0:T(2,128)(2,1)S(1)}, bf16[1,512]{1,0:T(2,128)(2,1)}, u32[]{:S(2)}) copy-start(bf16[1,512]{1,0:T(2,128)(2,1)} %param.24) | copy-start | bytes 3076
  5.6 9.6 %copy-start.11 = (f32[3,3,512]{2,1,0:T(4,128)S(1)}, f32[3,3,512]{2,1,0:T(4,128)}, u32[]{:S(2)}) copy-start(f32[3,3,512]{2,1,0:T(4,128)} %param.34) | copy-start | bytes 55300
  6.3 15.2 %copy-start.13 = (s32[64,16]{0,1:T(8,128)S(1)}, s32[64,16]{0,1:T(8,128)}, u32[]{:S(2)}) copy-start(s32[64,16]{0,1:T(8,128)} %param.27) | copy-start | bytes 12292
  6.3 16.4 %copy-start.20 = (s32[64,16]{0,1:T(8,128)S(1)}, s32[64,16]{0,1:T(8,128)}, u32[]{:S(2)}) copy-start(s32[64,16]{0,1:T(8,128)} %param.25) | copy-start | bytes 12292
  7.7 89.7 %collective-permute-start = (bf16[64,1024]{1,0:T(8,128)(2,1)S(1)}, bf16[64,1024]{1,0:T(8,128)(2,1)S(1)}, u32[]{:S(2)}, u32[]{:S(2)}) collective-permute-start(bf16[64,1024]{1,0:T(8,128)(2,1)S(1)} %pad_maximum_fusion.1), channel_id=1, source_target_pairs={{0,1},{1,2},{2,3},{3,4},{4,5},{5,6},{6,7},{7,8},{8,9},{9,10},{10,1... | collective-permute-start | bytes 393224 | tf_op jit(solution)/shard_map/ppermute | solution.py:16
  12.6 84.8 %collective-permute-start.1 = (bf16[64,1024]{1,0:T(8,128)(2,1)S(1)}, bf16[64,1024]{1,0:T(8,128)(2,1)}, u32[]{:S(2)}, u32[]{:S(2)}) collective-permute-start(bf16[64,1024]{1,0:T(8,128)(2,1)S(1)} %pad_maximum_fusion.1), channel_id=1, source_target_pairs={{1,0},{2,1},{3,2},{4,3},{5,4},{6,5},{7,6},{8,7},{9,8},{10,9},{11,1... | collective-permute-start | bytes 393224 | tf_op jit(solution)/shard_map/ppermute | solution.py:19
  24.5 2.2 %copy-start = (bf16[1024,512]{0,1:T(8,128)(2,1)}, bf16[1024,512]{0,1:T(8,128)(2,1)S(1)}, u32[]{:S(2)}) copy-start(bf16[1024,512]{0,1:T(8,128)(2,1)S(1)} %copy.175) | copy-start | bytes 3145732
  28.1 2.7 %copy-start.23 = (bf16[4,512]{1,0:T(4,128)(2,1)S(1)}, bf16[4,512]{1,0:T(4,128)(2,1)}, u32[]{:S(2)}) copy-start(bf16[4,512]{1,0:T(4,128)(2,1)} %param.23) | copy-start | bytes 12292
  28.1 2.8 %copy-start.24 = (f32[1,1,512]{2,1,0:T(1,128)S(1)}, f32[1,1,512]{2,1,0:T(1,128)}, u32[]{:S(2)}) copy-start(f32[1,1,512]{2,1,0:T(1,128)} %get-tuple-element.23) | copy-start | bytes 6148
  28.1 5.5 %copy-start.6 = (bf16[512,512]{0,1:T(8,128)(2,1)S(1)}, bf16[512,512]{0,1:T(8,128)(2,1)}, u32[]{:S(2)}) copy-start(bf16[512,512]{0,1:T(8,128)(2,1)} %get-tuple-element.15) | copy-start | bytes 1572868
  32.9 0.7 copy-start.15
  60.2 8.0 %copy-start.18 = (f32[1,512]{1,0:T(1,128)S(1)}, f32[1,512]{1,0:T(1,128)}, u32[]{:S(2)}) copy-start(f32[1,512]{1,0:T(1,128)} %fusion.70) | copy-start | bytes 6148
  60.2 20.3 %copy-start.12 = (s32[64,16]{0,1:T(8,128)S(1)}, s32[64,16]{0,1:T(8,128)}, u32[]{:S(2)}) copy-start(s32[64,16]{0,1:T(8,128)} %compare_select_fusion) | copy-start | bytes 12292
  60.2 20.5 %copy-start.19 = (pred[64,16]{0,1:T(8,128)(4,1)S(1)}, pred[64,16]{0,1:T(8,128)(4,1)}, u32[]{:S(2)}) copy-start(pred[64,16]{0,1:T(8,128)(4,1)} %compare_and_fusion) | copy-start | bytes 3076
  89.2 7.6 %copy-start.25 = (f32[3,8]{1,0:T(4,128)S(1)}, f32[3,8]{1,0:T(4,128)}, u32[]{:S(2)}) copy-start(f32[3,8]{1,0:T(4,128)} %param.35) | copy-start | bytes 292
  119.4 1.7 %copy-start.1 = (bf16[1024,512]{0,1:T(8,128)(2,1)S(1)}, bf16[1024,512]{0,1:T(8,128)(2,1)}, u32[]{:S(2)}) copy-start(bf16[1024,512]{0,1:T(8,128)(2,1)} %copy-done) | copy-start | bytes 3145732
  119.4 1.7 %copy-start.10 = (bf16[1,512,512]{2,1,0:T(8,128)(2,1)S(1)}, bf16[1,512,512]{2,1,0:T(8,128)(2,1)}, u32[]{:S(2)}) copy-start(bf16[1,512,512]{2,1,0:T(8,128)(2,1)} %get-tuple-element.13) | copy-start | bytes 1572868
  121.1 1.4 copy-start.17
  122.4 2.3 %copy-start.2 = (f32[1024,512]{0,1:T(8,128)}, f32[1024,512]{0,1:T(8,128)S(1)}, u32[]{:S(2)}) copy-start(f32[1024,512]{0,1:T(8,128)S(1)} %get-tuple-element.44) | copy-start | bytes 6291460
  125.0 1.1 copy-start.21
  125.0 1.1 copy-start.27
  126.1 4.3 %copy-start.4 = (bf16[1024,8,64]{2,1,0:T(8,128)(2,1)S(1)}, bf16[1024,8,64]{2,1,0:T(8,128)(2,1)}, u32[]{:S(2)}) copy-start(bf16[1024,8,64]{2,1,0:T(8,128)(2,1)} %gather_fusion.3) | copy-start | bytes 3145732
  130.5 2.1 %copy-start.3 = (f32[1024,512]{0,1:T(8,128)S(1)}, f32[1024,512]{0,1:T(8,128)}, u32[]{:S(2)}) copy-start(f32[1024,512]{0,1:T(8,128)} %copy-done.2) | copy-start | bytes 6291460
  130.5 2.1 %copy-start.9 = (bf16[1,512,512]{2,1,0:T(8,128)(2,1)S(1)}, bf16[1,512,512]{2,1,0:T(8,128)(2,1)}, u32[]{:S(2)}) copy-start(bf16[1,512,512]{2,1,0:T(8,128)(2,1)} %get-tuple-element.14) | copy-start | bytes 1572868
  132.6 1.4 copy-start.16
  136.1 1.8 %copy-start.22 = (pred[64,16]{1,0:T(8,128)(4,1)S(1)}, pred[64,16]{1,0:T(8,128)(4,1)}, u32[]{:S(2)}) copy-start(pred[64,16]{1,0:T(8,128)(4,1)} %copy.209) | copy-start | bytes 3076
  136.1 1.8 %copy-start.26 = (f32[8]{0:T(128)S(1)}, f32[8]{0:T(128)}, u32[]{:S(2)}) copy-start(f32[8]{0:T(128)} %get-tuple-element.32) | copy-start | bytes 100
  138.0 3.9 %copy-start.5 = (bf16[1024,8,64]{2,1,0:T(8,128)(2,1)S(1)}, bf16[1024,8,64]{2,1,0:T(8,128)(2,1)}, u32[]{:S(2)}) copy-start(bf16[1024,8,64]{2,1,0:T(8,128)(2,1)} %gather_fusion.5) | copy-start | bytes 3145732
  141.9 2.1 %copy-start.8 = (bf16[1,512,512]{2,1,0:T(8,128)(2,1)S(1)}, bf16[1,512,512]{2,1,0:T(8,128)(2,1)}, u32[]{:S(2)}) copy-start(bf16[1,512,512]{2,1,0:T(8,128)(2,1)} %get-tuple-element.12) | copy-start | bytes 1572868
where the time goes:
time: 147 us
  local copies, waits for them, and re-layouts  61.7 us (42%)
  matrix products  38.5 us (26%)
  blocking collectives  26.6 us (18%)
  other arithmetic  11.5 us (8%)
  starting transfers between devices  6.23 us (4%)
  between operations  2.11 us (1%)
    gather x3, local copies, waits for them, and re-layouts, mix_across_tiers(): key_picked = jnp.take(key_heads, tier_positions, axis=1)  23 us
    gather x3, local copies, waits for them, and re-layouts, mix_across_tiers(): value_picked = jnp.take(value_heads, tier_positions, axis=1)  22.8 us
    all_gather x1, blocking collectives, per_device(): lax.all_gather(project(renewed_two, 1, address_matrix, content_matrix, re...  14.4 us
    all_gather x1, blocking collectives, per_device(): lax.all_gather(project(renewed_three, 2, address_matrix, content_matrix,...  12.2 us
    dot_general x3, matrix products, mix_across_tiers(): jnp.einsum('hbid,hbjd->hbij', queries, key_picked, preferred_element_type...  9.67 us
    unnamed x3, matrix products  6.07 us
    dot_general x3, matrix products, mix_across_tiers(): jnp.einsum('hbij,hbjd->hbid', weights, value_picked, preferred_element_ty...  5.79 us
    dot_general x3, matrix products, refresh(): jnp.dot(hidden, shrink_matrix[tier_ordinal], preferred_element_type=jnp.f...  5.56 us
  transfers between devices with their start and end apart: 2, of which 0 were waited for; matrix products, arithmetic and copies ran while one was open for 38% of the time, Pallas kernels for 0%

commit v1 on v0

v1 whole, which is shorter than its diff:
```python
import functools
import math

import jax
import jax.numpy as jnp
from jax import lax
from jax.experimental import pallas as pl
from jax.experimental.pallas import tpu as pltpu
from jax.sharding import PartitionSpec as P

eps = 1e-06
F32 = jnp.float32
BF16 = jnp.bfloat16
MESH = pl.DeviceIdType.MESH
NT = (((1,), (1,)), ((), ()))
SLOT = 8


def mm(a, b):
    return jnp.dot(a, b, preferred_element_type=F32)


def mm_nt(a, b):
    return lax.dot_general(a, b, NT, preferred_element_type=F32)


def iota(shape, dim):
    return lax.broadcasted_iota(jnp.int32, shape, dim)


def normalize(v, gain):
    return v * lax.rsqrt(jnp.mean(v * v, axis=-1, keepdims=True) + eps) * gain


def head_norm(v, mean_mat):
    half = mean_mat.shape[0]
    parts = []
    for at in range(0, v.shape[1], half):
        piece = v[:, at : at + half]
        mean = mm((piece * piece).astype(BF16), mean_mat)
        parts.append(piece * lax.rsqrt(mean + eps))
    return jnp.concatenate(parts, axis=1)


def expand_rows(counts, times):
    blocks, width = counts.shape
    return jnp.broadcast_to(counts[:, None, :], (blocks, times, width)).reshape(
        blocks * times, width
    )


def count_picks(picks, base, table, width):
    blocks, entries = picks.shape
    lane = iota((blocks, width), 1) % table
    total = jnp.zeros((blocks, width), F32)
    for j in range(entries):
        local = picks[:, j : j + 1] - base
        total = total + jnp.where(lane == local, 1.0, 0.0)
    return total


def kernel(
    sph_n, grp_n, heads, tile,
    x_hbm, c1_hbm, c2_ref, c3_ref, p1_ref, p2_ref, p3_ref,
    probe_hbm, address_hbm, content_hbm, merge_hbm, expand_hbm, shrink_hbm,
    gain_ref, scale_ref,
    out_hbm,
    x_v, q_v, out_v, tab1, slots2, slots3,
    probe, address, content, merge, expand, shrink,
    kq1, vq1, kb2, vb2, kb3, vb3, cnt1, cnt2, cnt3,
    w_sem, x_sem, out_sem, own_sem, s1_sem, r1_sem, s2_sem, r2_sem, s3_sem, r3_sem,
):
    rows, feature = x_v.shape
    block = c1_hbm.shape[0]
    group = rows // block
    hd = feature // heads
    quad = 4
    quads = heads // quad
    qf = quad * hd
    n2, n3 = c2_ref.shape[0], c3_ref.shape[0]
    t1, t2, t3 = tab1.shape[0], n2 * grp_n, n3 * sph_n
    sph, grp = lax.axis_index("sph"), lax.axis_index("grp")
    me = sph * grp_n + grp
    count = sph_n * grp_n
    right, left = (me + 1) % count, (me + count - 1) % count
    right_id = (right // grp_n, right % grp_n)
    left_id = (left // grp_n, left % grp_n)
    grp_ids = [(sph, (grp + k) % grp_n) for k in range(1, grp_n)]
    sph_ids = [((sph + k) % sph_n, grp) for k in range(1, sph_n)]

    barrier = pltpu.get_barrier_semaphore()
    for who in [right_id, left_id] + grp_ids + sph_ids:
        pl.semaphore_signal(barrier, inc=1, device_id=who, device_id_type=MESH)

    x_copy = pltpu.make_async_copy(x_hbm, x_v, x_sem)
    x_copy.start()
    own = pltpu.make_async_copy(c1_hbm, tab1.at[pl.ds(block, block)], own_sem)
    own.start()
    w_copies = {}
    pairs = {
        "probe": (probe_hbm, probe), "expand": (expand_hbm, expand),
        "shrink": (shrink_hbm, shrink), "address": (address_hbm, address),
        "content": (content_hbm, content), "merge": (merge_hbm, merge),
    }
    order = [("probe", 0)]
    for level in (1, 2):
        order += [(n, level) for n in ("expand", "shrink", "address", "content", "merge")]
    order += [(n, 0) for n in ("expand", "shrink", "address", "content", "merge")]
    order += [("probe", 1), ("probe", 2)]
    for i, (name, level) in enumerate(order):
        src, dst = pairs[name]
        cp = pltpu.make_async_copy(src.at[level], dst.at[level], w_sem.at[i])
        cp.start()
        w_copies[name, level] = cp

    slots2[grp] = jnp.concatenate(
        [c2_ref[...].astype(F32), jnp.zeros((SLOT - n2, feature), F32)], axis=0
    )
    slots3[sph] = jnp.concatenate(
        [c3_ref[...].astype(F32), jnp.zeros((SLOT - n3, feature), F32)], axis=0
    )

    pl.semaphore_wait(barrier, 2 + len(grp_ids) + len(sph_ids))
    remote = []
    for k, (who, lo) in enumerate(((right_id, 0), (left_id, 2 * block))):
        remote.append(pltpu.make_async_remote_copy(
            src_ref=c1_hbm, dst_ref=tab1.at[pl.ds(lo, block)],
            send_sem=s1_sem.at[k], recv_sem=r1_sem.at[k],
            device_id=who, device_id_type=MESH))
    for k, who in enumerate(grp_ids):
        remote.append(pltpu.make_async_remote_copy(
            src_ref=slots2.at[grp], dst_ref=slots2.at[grp],
            send_sem=s2_sem.at[k], recv_sem=r2_sem.at[k],
            device_id=who, device_id_type=MESH))
    for k, who in enumerate(sph_ids):
        remote.append(pltpu.make_async_remote_copy(
            src_ref=slots3.at[sph], dst_ref=slots3.at[sph],
            send_sem=s3_sem.at[k], recv_sem=r3_sem.at[k],
            device_id=who, device_id_type=MESH))
    for cp in remote:
        cp.start()

    mean_mat = jnp.where(
        iota((qf, qf), 0) // hd == iota((qf, qf), 1) // hd, 1.0 / hd, 0.0
    ).astype(BF16)

    cnt1[...] = count_picks(p1_ref[...], (me - 1) * block, t1, quad * t1)
    cnt2[...] = count_picks(p2_ref[...], sph * t2, t2, heads * t2)
    cnt3[...] = count_picks(p3_ref[...], 0, t3, heads * t3)

    x_copy.wait()
    w_copies["probe", 0].wait()

    def query(state, level):
        normed = normalize(state, gain_ref[level, 0:1, :]).astype(BF16)
        return head_norm(mm(normed, probe[level]), mean_mat).astype(BF16)

    def first_query(i, carry):
        at = pl.ds(pl.multiple_of(i * tile, tile), tile)
        q_v[at, :] = query(x_v[at, :].astype(F32), 0)
        return carry

    lax.fori_loop(0, rows // tile, first_query, 0)

    def scale_row(level):
        head = iota((1, feature), 1) // hd
        row = jnp.zeros((1, feature), F32)
        for h in range(heads):
            row = jnp.where(head == h, scale_ref[level, h], row)
        return row * (math.log2(math.e) / math.sqrt(hd))

    def latents(latent, level):
        for name in ("expand", "shrink", "address", "content"):
            w_copies[name, level].wait()
        mlp_in = normalize(latent, gain_ref[level, 1:2, :]).astype(BF16)
        hidden = mm(mlp_in, expand[level])
        hidden = (hidden / (1.0 + jnp.exp(-hidden))).astype(BF16)
        renewed = (latent + mm(hidden, shrink[level])).astype(BF16).astype(F32)
        kv_in = normalize(renewed, gain_ref[level, 2:3, :]).astype(BF16)
        key = head_norm(mm(kv_in, address[level]), mean_mat) * scale_row(level)
        return key, mm(kv_in, content[level])

    def compact(slots, n, table):
        count = slots.shape[0]
        flat = slots[...].reshape(count * SLOT, feature).astype(BF16)
        padded = max(table, 16)
        row, col = iota((padded, count * SLOT), 0), iota((padded, count * SLOT), 1)
        pick = jnp.where(col == row // n * SLOT + row % n, 1.0, 0.0).astype(BF16)
        return mm(pick, flat)

    def by_head(v, table, count):
        stacked = jnp.concatenate([v[:table]] * count, axis=0)
        mask = iota(stacked.shape, 0) // table == iota(stacked.shape, 1) // hd
        return jnp.where(mask, stacked, 0.0).astype(BF16)

    def small_level(slots, n, table, level, kb, vb):
        key, value = latents(compact(slots, n, table), level)
        kb[...] = by_head(key, table, heads)
        w_copies["merge", level].wait()
        vb[...] = mm(by_head(value, table, heads), merge[level]).astype(BF16)

    for cp in remote[2 : 2 + len(grp_ids)]:
        cp.wait_recv()
    small_level(slots2, n2, t2, 1, kb2, vb2)
    for cp in remote[2 + len(grp_ids) :]:
        cp.wait_recv()
    small_level(slots3, n3, t3, 2, kb3, vb3)
    own.wait()
    for cp in remote[:2]:
        cp.wait_recv()
    key, value = latents(tab1[...].astype(F32), 0)
    for a in range(quads):
        kq1[a] = by_head(key[:, a * qf : (a + 1) * qf], t1, quad)
        vq1[a, :, :qf] = by_head(value[:, a * qf : (a + 1) * qf], t1, quad)
        vq1[a, :, qf:] = by_head(jnp.ones((t1, qf), F32), t1, quad)
    w_copies["merge", 0].wait()
    w_copies["probe", 1].wait()
    w_copies["probe", 2].wait()

    def sum_mat(table):
        width = heads * table
        return jnp.where(
            iota((width, width), 0) // table == iota((width, width), 1) // table, 1.0, 0.0
        ).astype(BF16)

    sum2, sum3 = sum_mat(t2), sum_mat(t3)

    def small_mix(state, level, kb, vb, counts, sums):
        q = query(state, level)
        p = jnp.exp2(mm_nt(q, kb[...])) * counts
        total = mm(p.astype(BF16), sums)
        return state + mm((p / total).astype(BF16), vb[...])

    tb = tile // group

    def out_copy(i):
        at = pl.ds(pl.multiple_of(i * tile, tile), tile)
        return pltpu.make_async_copy(out_v.at[at], out_hbm.at[at], out_sem.at[i])

    def fine(i, carry):
        at = pl.ds(pl.multiple_of(i * tile, tile), tile)
        bt = pl.ds(pl.multiple_of(i * tb, tb), tb)
        state = x_v[at, :].astype(F32)
        counts = expand_rows(cnt1[bt, :], group)
        mixed = []
        for a in range(quads):
            p = jnp.exp2(mm_nt(q_v[at, a * qf : (a + 1) * qf], kq1[a])) * counts
            o = mm(p.astype(BF16), vq1[a])
            mixed.append((o[:, :qf] / o[:, qf:]).astype(BF16))
        state = state + mm(jnp.concatenate(mixed, axis=1), merge[0])
        state = small_mix(state, 1, kb2, vb2, expand_rows(cnt2[bt, :], group), sum2)
        state = small_mix(state, 2, kb3, vb3, expand_rows(cnt3[bt, :], group), sum3)
        out_v[at, :] = state.astype(BF16)
        out_copy(i).start()
        return carry

    lax.fori_loop(0, rows // tile, fine, 0)
    for i in range(rows // tile):
        out_copy(i).wait()
    for cp in remote:
        cp.wait_send()


def per_device(sph_n, grp_n, *args):
    (x, c1, c2, c3, p1, p2, p3, probe, address, content, merge, expand, shrink, gain, scale) = args
    rows, feature = x.shape
    levels, heads = scale.shape
    block = c1.shape[0]
    tile = 256
    t1, t2, t3 = 3 * block, c2.shape[0] * grp_n, c3.shape[0] * sph_n
    hd = feature // heads
    qf = 4 * hd
    quads = heads // 4
    any_ = pl.BlockSpec(memory_space=pl.ANY)
    vmem = pl.BlockSpec(memory_space=pltpu.VMEM)
    smem = pl.BlockSpec(memory_space=pltpu.SMEM)
    dma = pltpu.SemaphoreType.DMA
    return pl.pallas_call(
        functools.partial(kernel, sph_n, grp_n, heads, tile),
        out_shape=jax.ShapeDtypeStruct((rows, feature), BF16),
        in_specs=[any_, any_, vmem, vmem, vmem, vmem, vmem] + [any_] * 6 + [vmem, smem],
        out_specs=any_,
        scratch_shapes=[
            pltpu.VMEM((rows, feature), BF16),
            pltpu.VMEM((rows, feature), BF16),
            pltpu.VMEM((rows, feature), BF16),
            pltpu.VMEM((t1, feature), BF16),
            pltpu.VMEM((grp_n, SLOT, feature), F32),
            pltpu.VMEM((sph_n, SLOT, feature), F32),
            pltpu.VMEM(probe.shape, BF16),
            pltpu.VMEM(address.shape, BF16),
            pltpu.VMEM(content.shape, BF16),
            pltpu.VMEM(merge.shape, BF16),
            pltpu.VMEM(expand.shape, BF16),
            pltpu.VMEM(shrink.shape, BF16),
            pltpu.VMEM((quads, 4 * t1, qf), BF16),
            pltpu.VMEM((quads, 4 * t1, 2 * qf), BF16),
            pltpu.VMEM((heads * t2, feature), BF16),
            pltpu.VMEM((heads * t2, feature), BF16),
            pltpu.VMEM((heads * t3, feature), BF16),
            pltpu.VMEM((heads * t3, feature), BF16),
            pltpu.VMEM((block, 4 * t1), F32),
            pltpu.VMEM((block, heads * t2), F32),
            pltpu.VMEM((block, heads * t3), F32),
            dma((6 * levels,)), dma, dma((rows // tile,)), dma,
            dma((2,)), dma((2,)),
            dma((grp_n - 1,)), dma((grp_n - 1,)),
            dma((sph_n - 1,)), dma((sph_n - 1,)),
        ],
        compiler_params=pltpu.CompilerParams(
            collective_id=0, has_side_effects=True, vmem_limit_bytes=56 * 1024 * 1024
        ),
    )(x, c1, c2, c3, p1, p2, p3, probe, address, content, merge, expand, shrink, gain, scale)


def solution(mesh):
    both = P(("sph", "grp"), None)
    placed = (both, both, both, P("sph", None), both, both, both) + (P(),) * 8
    return jax.shard_map(
        functools.partial(per_device, mesh.shape["sph"], mesh.shape["grp"]),
        mesh=mesh, in_specs=placed, out_specs=both, check_vma=False,
    )
```

time: 147 us -> 36.8 us (0.25)
  local copies, waits for them, and re-layouts: 61.7 us -> 6.42 us
  matrix products: 38.5 us -> 0 us
  Pallas kernels: 0 us -> 30 us
  blocking collectives: 26.6 us -> 0 us
  other arithmetic: 11.5 us -> 0 us
  starting transfers between devices: 6.23 us -> 0 us
  between operations: 2.11 us -> 0.01 us
    gather x6 -> x0, local copies, waits for them, and re-layouts: 45.8 us -> none  [the longest x3 23 us: mix_across_tiers(): key_picked = jnp.take(key_heads, tier_positions, axis=1)]
    dot_general x19 -> x0, matrix products: 32.4 us -> none  [the longest x3 9.67 us: mix_across_tiers(): jnp.einsum('hbid,hbjd->hbij', queries, key_picked, preferred_element_type...]
    pallas_call x0 -> x1, Pallas kernels: none -> 30 us  [per_device(): pl.pallas_call(functools.partial(kernel, sph_n, grp_n, heads, tile), out_...]
    all_gather x2 -> x0, blocking collectives: 26.6 us -> none  [the longest x1 14.4 us: per_device(): lax.all_gather(project(renewed_two, 1, address_matrix, content_matrix, re...]
    ppermute x2 -> x0, starting transfers between devices: 6.23 us -> none  [the longest x1 4.93 us: with_halo(): lax.ppermute(lax.slice_in_dim(block, block.shape[dim] - width, None, axis...]
    unnamed x3 -> x0, matrix products: 6.07 us -> none
    convert_element_type x10 -> x0, local copies, waits for them, and re-layouts: 5.49 us -> none  [the longest x3 3.95 us: mix_across_tiers(): queries.astype(jnp.bfloat16)]
    unnamed x59 -> x4, local copies, waits for them, and re-layouts: 1.63 us -> 6.42 us
  transfers between devices with their start and end apart: 2 -> 0, of which waited for: 0 -> 0; matrix products, arithmetic and copies ran while one was open for 38% -> 0% of each run, Pallas kernels for 0% -> 0%
where the time goes in v1:
time: 36.8 us; the launch traced here: 36.4 us
  Pallas kernels  30 us (82%)
  local copies, waits for them, and re-layouts  6.42 us (17%)
    pallas_call x1, Pallas kernels, per_device(): pl.pallas_call(functools.partial(kernel, sph_n, grp_n, heads, tile), out_...  30 us
    unnamed x4, local copies, waits for them, and re-layouts  6.42 us

profile of v1, /device:TPU:0, one launch (start us, length us, event | category | flops | bytes accessed | tf_op | source)
XLA Modules:
  0.0 36.4 jit_solution(12050726752260915500)
XLA Ops:
  0.0 1.4 %copy.16.p1_ref = s32[64,16]{1,0:T(8,128)} copy(s32[64,16]{0,1:T(8,128)} %param.19) | data formatting | bytes 8192 | tf_op args[4]
  1.4 1.4 %copy.17.p2_ref = s32[64,16]{1,0:T(8,128)} copy(s32[64,16]{0,1:T(8,128)} %param.20) | data formatting | bytes 8192 | tf_op args[5]
  2.8 1.4 %copy.18.p3_ref = s32[64,16]{1,0:T(8,128)} copy(s32[64,16]{0,1:T(8,128)} %param.21) | data formatting | bytes 8192 | tf_op args[6]
  4.2 30.0 %shard_map.145 = bf16[1024,512]{1,0:T(8,128)(2,1)} custom-call(bf16[1024,512]{1,0:T(8,128)(2,1)} %x_hbm.1, bf16[64,512]{1,0:T(8,128)(2,1)} %c1_hbm.1, bf16[4,512]{1,0:T(4,128)(2,1)} %c2_ref.1, bf16[1,512]{1,0:T(2,128)(2,1)} %c3_ref.1, s32[64,16]{1,0:T(8,128)} %copy.16.p1_ref, s32[64,16]{1,0:T(8,128)} %copy.17.p2_ref, s32[64,16]{1,0:T(8,128)} %copy.18.p3_ref, ...), custom_call_target="tpu_custom_call" | custom-call | tf_op jit(solution)/shard_map/pallas_call | solution.py:278
  34.2 2.3 %copy.20 = bf16[1024,512]{1,0:T(8,128)(2,1)} copy(bf16[1024,512]{1,0:T(8,128)(2,1)} %shard_map.145) | data formatting | bytes 2097152

commit v2 on v1

--- a/solution.py
+++ b/solution.py
@@ -13,7 +13,6 @@
 BF16 = jnp.bfloat16
 MESH = pl.DeviceIdType.MESH
 NT = (((1,), (1,)), ((), ()))
-SLOT = 8
 
 
 def mm(a, b):
@@ -49,26 +48,28 @@
     )
 
 
-def count_picks(picks, base, table, width):
+def count_picks(picks_t, base, table, width):
+    picks = jnp.transpose((picks_t - base).astype(F32)).astype(jnp.int32)
     blocks, entries = picks.shape
     lane = iota((blocks, width), 1) % table
     total = jnp.zeros((blocks, width), F32)
     for j in range(entries):
-        local = picks[:, j : j + 1] - base
+        local = picks[:, j : j + 1]
         total = total + jnp.where(lane == local, 1.0, 0.0)
     return total
 
 
 def kernel(
     sph_n, grp_n, heads, tile,
-    x_hbm, c1_hbm, c2_ref, c3_ref, p1_ref, p2_ref, p3_ref,
+    x_hbm, c1_hbm, c2_hbm, c3_hbm, p1_hbm, p2_hbm, p3_hbm,
     probe_hbm, address_hbm, content_hbm, merge_hbm, expand_hbm, shrink_hbm,
-    gain_ref, scale_ref,
-    out_hbm,
-    x_v, q_v, out_v, tab1, slots2, slots3,
+    gain_hbm, scale_hbm,
+    out_ref,
+    c2_ref, c3_ref, p1_ref, p2_ref, p3_ref, gain_ref, scale_ref,
+    x_v, q_v, tab1, slots2, slots3,
     probe, address, content, merge, expand, shrink,
     kq1, vq1, kb2, vb2, kb3, vb3, cnt1, cnt2, cnt3,
-    w_sem, x_sem, out_sem, own_sem, s1_sem, r1_sem, s2_sem, r2_sem, s3_sem, r3_sem,
+    in_sem, w_sem, x_sem, own_sem, s1_sem, r1_sem, s2_sem, r2_sem, s3_sem, r3_sem,
 ):
     rows, feature = x_v.shape
     block = c1_hbm.shape[0]
@@ -77,7 +78,7 @@
     quad = 4
     quads = heads // quad
     qf = quad * hd
-    n2, n3 = c2_ref.shape[0], c3_ref.shape[0]
+    n2, n3 = c2_hbm.shape[0], c3_hbm.shape[0]
     t1, t2, t3 = tab1.shape[0], n2 * grp_n, n3 * sph_n
     sph, grp = lax.axis_index("sph"), lax.axis_index("grp")
     me = sph * grp_n + grp
@@ -92,6 +93,14 @@
     for who in [right_id, left_id] + grp_ids + sph_ids:
         pl.semaphore_signal(barrier, inc=1, device_id=who, device_id_type=MESH)
 
+    small = []
+    for i, (src, dst) in enumerate((
+        (c3_hbm, c3_ref), (c2_hbm, c2_ref), (gain_hbm, gain_ref), (p1_hbm, p1_ref),
+        (p2_hbm, p2_ref), (p3_hbm, p3_ref), (scale_hbm, scale_ref),
+    )):
+        cp = pltpu.make_async_copy(src, dst, in_sem.at[i])
+        cp.start()
+        small.append(cp)
     x_copy = pltpu.make_async_copy(x_hbm, x_v, x_sem)
     x_copy.start()
     own = pltpu.make_async_copy(c1_hbm, tab1.at[pl.ds(block, block)], own_sem)
@@ -109,16 +118,15 @@
     order += [("probe", 1), ("probe", 2)]
     for i, (name, level) in enumerate(order):
         src, dst = pairs[name]
-        cp = pltpu.make_async_copy(src.at[level], dst.at[level], w_sem.at[i])
-        cp.start()
-        w_copies[name, level] = cp
-
-    slots2[grp] = jnp.concatenate(
-        [c2_ref[...].astype(F32), jnp.zeros((SLOT - n2, feature), F32)], axis=0
-    )
-    slots3[sph] = jnp.concatenate(
-        [c3_ref[...].astype(F32), jnp.zeros((SLOT - n3, feature), F32)], axis=0
-    )
+        w_copies[name, level] = pltpu.make_async_copy(
+            src.at[level], dst.at[level], w_sem.at[i]
+        )
+    w_copies["probe", 0].start()
+
+    small[0].wait()
+    small[1].wait()
+    slots2[grp] = c2_ref[...].astype(F32)
+    slots3[sph] = c3_ref[...].astype(F32)
 
     pl.semaphore_wait(barrier, 2 + len(grp_ids) + len(sph_ids))
     remote = []
@@ -139,6 +147,10 @@
             device_id=who, device_id_type=MESH))
     for cp in remote:
         cp.start()
+    for key in order[1:]:
+        w_copies[key].start()
+    for cp in small[2:]:
+        cp.wait()
 
     mean_mat = jnp.where(
         iota((qf, qf), 0) // hd == iota((qf, qf), 1) // hd, 1.0 / hd, 0.0
@@ -166,7 +178,7 @@
         head = iota((1, feature), 1) // hd
         row = jnp.zeros((1, feature), F32)
         for h in range(heads):
-            row = jnp.where(head == h, scale_ref[level, h], row)
+            row = jnp.where(head == h, scale_ref[level : level + 1, h : h + 1], row)
         return row * (math.log2(math.e) / math.sqrt(hd))
 
     def latents(latent, level):
@@ -180,31 +192,29 @@
         key = head_norm(mm(kv_in, address[level]), mean_mat) * scale_row(level)
         return key, mm(kv_in, content[level])
 
-    def compact(slots, n, table):
-        count = slots.shape[0]
-        flat = slots[...].reshape(count * SLOT, feature).astype(BF16)
-        padded = max(table, 16)
-        row, col = iota((padded, count * SLOT), 0), iota((padded, count * SLOT), 1)
-        pick = jnp.where(col == row // n * SLOT + row % n, 1.0, 0.0).astype(BF16)
-        return mm(pick, flat)
+    def compact(slots, table):
+        pieces = [slots[k] for k in range(slots.shape[0])]
+        if table < 16:
+            pieces.append(jnp.zeros((16 - table, feature), F32))
+        return jnp.concatenate(pieces, axis=0)
 
     def by_head(v, table, count):
         stacked = jnp.concatenate([v[:table]] * count, axis=0)
         mask = iota(stacked.shape, 0) // table == iota(stacked.shape, 1) // hd
         return jnp.where(mask, stacked, 0.0).astype(BF16)
 
-    def small_level(slots, n, table, level, kb, vb):
-        key, value = latents(compact(slots, n, table), level)
+    def small_level(slots, table, level, kb, vb):
+        key, value = latents(compact(slots, table), level)
         kb[...] = by_head(key, table, heads)
         w_copies["merge", level].wait()
         vb[...] = mm(by_head(value, table, heads), merge[level]).astype(BF16)
 
     for cp in remote[2 : 2 + len(grp_ids)]:
         cp.wait_recv()
-    small_level(slots2, n2, t2, 1, kb2, vb2)
+    small_level(slots2, t2, 1, kb2, vb2)
     for cp in remote[2 + len(grp_ids) :]:
         cp.wait_recv()
-    small_level(slots3, n3, t3, 2, kb3, vb3)
+    small_level(slots3, t3, 2, kb3, vb3)
     own.wait()
     for cp in remote[:2]:
         cp.wait_recv()
@@ -232,10 +242,6 @@
         return state + mm((p / total).astype(BF16), vb[...])
 
     tb = tile // group
-
-    def out_copy(i):
-        at = pl.ds(pl.multiple_of(i * tile, tile), tile)
-        return pltpu.make_async_copy(out_v.at[at], out_hbm.at[at], out_sem.at[i])
 
     def fine(i, carry):
         at = pl.ds(pl.multiple_of(i * tile, tile), tile)
@@ -250,13 +256,10 @@
         state = state + mm(jnp.concatenate(mixed, axis=1), merge[0])
         state = small_mix(state, 1, kb2, vb2, expand_rows(cnt2[bt, :], group), sum2)
         state = small_mix(state, 2, kb3, vb3, expand_rows(cnt3[bt, :], group), sum3)
-        out_v[at, :] = state.astype(BF16)
-        out_copy(i).start()
+        out_ref[at, :] = state.astype(BF16)
         return carry
 
     lax.fori_loop(0, rows // tile, fine, 0)
-    for i in range(rows // tile):
-        out_copy(i).wait()
     for cp in remote:
         cp.wait_send()
 
@@ -272,21 +275,25 @@
     qf = 4 * hd
     quads = heads // 4
     any_ = pl.BlockSpec(memory_space=pl.ANY)
-    vmem = pl.BlockSpec(memory_space=pltpu.VMEM)
-    smem = pl.BlockSpec(memory_space=pltpu.SMEM)
     dma = pltpu.SemaphoreType.DMA
     return pl.pallas_call(
         functools.partial(kernel, sph_n, grp_n, heads, tile),
-        out_shape=jax.ShapeDtypeStruct((rows, feature), BF16),
-        in_specs=[any_, any_, vmem, vmem, vmem, vmem, vmem] + [any_] * 6 + [vmem, smem],
-        out_specs=any_,
+        out_shape=pltpu.VMEM((rows, feature), BF16),
+        in_specs=[any_] * 15,
+        out_specs=pl.BlockSpec(memory_space=pltpu.VMEM),
         scratch_shapes=[
-            pltpu.VMEM((rows, feature), BF16),
+            pltpu.VMEM(c2.shape, BF16),
+            pltpu.VMEM(c3.shape, BF16),
+            pltpu.VMEM(p1.shape[::-1], jnp.int32),
+            pltpu.VMEM(p2.shape[::-1], jnp.int32),
+            pltpu.VMEM(p3.shape[::-1], jnp.int32),
+            pltpu.VMEM(gain.shape, F32),
+            pltpu.VMEM(scale.shape, F32),
             pltpu.VMEM((rows, feature), BF16),
             pltpu.VMEM((rows, feature), BF16),
             pltpu.VMEM((t1, feature), BF16),
-            pltpu.VMEM((grp_n, SLOT, feature), F32),
-            pltpu.VMEM((sph_n, SLOT, feature), F32),
+            pltpu.VMEM((grp_n,) + c2.shape, F32),
+            pltpu.VMEM((sph_n,) + c3.shape, F32),
             pltpu.VMEM(probe.shape, BF16),
             pltpu.VMEM(address.shape, BF16),
             pltpu.VMEM(content.shape, BF16),
@@ -302,15 +309,15 @@
             pltpu.VMEM((block, 4 * t1), F32),
             pltpu.VMEM((block, heads * t2), F32),
             pltpu.VMEM((block, heads * t3), F32),
-            dma((6 * levels,)), dma, dma((rows // tile,)), dma,
+            dma((7,)), dma((6 * levels,)), dma, dma,
             dma((2,)), dma((2,)),
             dma((grp_n - 1,)), dma((grp_n - 1,)),
             dma((sph_n - 1,)), dma((sph_n - 1,)),
         ],
         compiler_params=pltpu.CompilerParams(
-            collective_id=0, has_side_effects=True, vmem_limit_bytes=56 * 1024 * 1024
+            collective_id=0, has_side_effects=True, vmem_limit_bytes=122 * 512 * 1024
         ),
-    )(x, c1, c2, c3, p1, p2, p3, probe, address, content, merge, expand, shrink, gain, scale)
+    )(x, c1, c2, c3, p1.T, p2.T, p3.T, probe, address, content, merge, expand, shrink, gain, scale)
 
 
 def solution(mesh):

time: 36.8 us -> 28.9 us (0.79)
  local copies, waits for them, and re-layouts: 6.42 us -> 0.97 us
  Pallas kernels: 30 us -> 27.8 us
    unnamed x4 -> x1, local copies, waits for them, and re-layouts: 6.42 us -> 0.97 us
    pallas_call x1, Pallas kernels: 30 us -> 27.8 us  [per_device(): pl.pallas_call(functools.partial(kernel, sph_n, grp_n, heads, tile), out_...]
where the time goes in v2:
time: 28.9 us; the launch traced here: 28.7 us
  Pallas kernels  27.8 us (96%)
  local copies, waits for them, and re-layouts  0.97 us (3%)
    pallas_call x1, Pallas kernels, per_device(): pl.pallas_call(functools.partial(kernel, sph_n, grp_n, heads, tile), out_...  27.8 us
    unnamed x1, local copies, waits for them, and re-layouts  0.97 us

profile of v2, /device:TPU:0, one launch (start us, length us, event | category | flops | bytes accessed | tf_op | source)
XLA Modules:
  0.0 28.7 jit_solution(10368863150627421558)
XLA Ops:
  0.0 27.8 %shard_map.145 = bf16[1024,512]{1,0:T(8,128)(2,1)S(1)} custom-call(bf16[1024,512]{1,0:T(8,128)(2,1)} %x_hbm.1, bf16[64,512]{1,0:T(8,128)(2,1)} %c1_hbm.1, bf16[4,512]{1,0:T(4,128)(2,1)} %c2_hbm.1, bf16[1,512]{1,0:T(2,128)(2,1)} %c3_hbm.1, s32[16,64]{1,0:T(8,128)} %bitcast.3, s32[16,64]{1,0:T(8,128)} %bitcast.4, s32[16,64]{1,0:T(8,128)} %bitcast.5, ...), custom_call_target="tpu_custom_call" | custom-call | tf_op jit(solution)/shard_map/pallas_call | solution.py:279
  27.8 1.0 %copy.17 = bf16[1024,512]{1,0:T(8,128)(2,1)} copy(bf16[1024,512]{1,0:T(8,128)(2,1)S(1)} %shard_map.145) | data formatting | bytes 2097152

commit v3 on v2

--- a/solution.py
+++ b/solution.py
@@ -205,7 +205,7 @@
 
     def small_level(slots, table, level, kb, vb):
         key, value = latents(compact(slots, table), level)
-        kb[...] = by_head(key, table, heads)
+        kb[...] = by_head(key, table, heads).T
         w_copies["merge", level].wait()
         vb[...] = mm(by_head(value, table, heads), merge[level]).astype(BF16)
 
@@ -220,7 +220,7 @@
         cp.wait_recv()
     key, value = latents(tab1[...].astype(F32), 0)
     for a in range(quads):
-        kq1[a] = by_head(key[:, a * qf : (a + 1) * qf], t1, quad)
+        kq1[a] = by_head(key[:, a * qf : (a + 1) * qf], t1, quad).T
         vq1[a, :, :qf] = by_head(value[:, a * qf : (a + 1) * qf], t1, quad)
         vq1[a, :, qf:] = by_head(jnp.ones((t1, qf), F32), t1, quad)
     w_copies["merge", 0].wait()
@@ -237,9 +237,9 @@
 
     def small_mix(state, level, kb, vb, counts, sums):
         q = query(state, level)
-        p = jnp.exp2(mm_nt(q, kb[...])) * counts
+        p = jnp.exp2(mm(q, kb[...])) * counts
         total = mm(p.astype(BF16), sums)
-        return state + mm((p / total).astype(BF16), vb[...])
+        return state + mm((p * pl.reciprocal(total, approx=True)).astype(BF16), vb[...])
 
     tb = tile // group
 
@@ -250,9 +250,9 @@
         counts = expand_rows(cnt1[bt, :], group)
         mixed = []
         for a in range(quads):
-            p = jnp.exp2(mm_nt(q_v[at, a * qf : (a + 1) * qf], kq1[a])) * counts
+            p = jnp.exp2(mm(q_v[at, a * qf : (a + 1) * qf], kq1[a])) * counts
             o = mm(p.astype(BF16), vq1[a])
-            mixed.append((o[:, :qf] / o[:, qf:]).astype(BF16))
+            mixed.append((o[:, :qf] * pl.reciprocal(o[:, qf:], approx=True)).astype(BF16))
         state = state + mm(jnp.concatenate(mixed, axis=1), merge[0])
         state = small_mix(state, 1, kb2, vb2, expand_rows(cnt2[bt, :], group), sum2)
         state = small_mix(state, 2, kb3, vb3, expand_rows(cnt3[bt, :], group), sum3)
@@ -269,7 +269,7 @@
     rows, feature = x.shape
     levels, heads = scale.shape
     block = c1.shape[0]
-    tile = 256
+    tile = rows
     t1, t2, t3 = 3 * block, c2.shape[0] * grp_n, c3.shape[0] * sph_n
     hd = feature // heads
     qf = 4 * hd
@@ -300,11 +300,11 @@
             pltpu.VMEM(merge.shape, BF16),
             pltpu.VMEM(expand.shape, BF16),
             pltpu.VMEM(shrink.shape, BF16),
-            pltpu.VMEM((quads, 4 * t1, qf), BF16),
+            pltpu.VMEM((quads, qf, 4 * t1), BF16),
             pltpu.VMEM((quads, 4 * t1, 2 * qf), BF16),
+            pltpu.VMEM((feature, heads * t2), BF16),
             pltpu.VMEM((heads * t2, feature), BF16),
-            pltpu.VMEM((heads * t2, feature), BF16),
-            pltpu.VMEM((heads * t3, feature), BF16),
+            pltpu.VMEM((feature, heads * t3), BF16),
             pltpu.VMEM((heads * t3, feature), BF16),
             pltpu.VMEM((block, 4 * t1), F32),
             pltpu.VMEM((block, heads * t2), F32),

time: 28.9 us -> 24.5 us (0.85)
  Pallas kernels: 27.8 us -> 23.3 us
    pallas_call x1, Pallas kernels: 27.8 us -> 23.3 us  [per_device(): pl.pallas_call(functools.partial(kernel, sph_n, grp_n, heads, tile), out_...]
where the time goes in v3:
time: 24.5 us; the launch traced here: 24.3 us
  Pallas kernels  23.3 us (95%)
  local copies, waits for them, and re-layouts  0.97 us (4%)
    pallas_call x1, Pallas kernels, per_device(): pl.pallas_call(functools.partial(kernel, sph_n, grp_n, heads, tile), out_...  23.3 us
    unnamed x1, local copies, waits for them, and re-layouts  0.97 us

profile of v3, /device:TPU:0, one launch (start us, length us, event | category | flops | bytes accessed | tf_op | source)
XLA Modules:
  0.0 24.3 jit_solution(8547594359347499655)
XLA Ops:
  0.0 23.3 %shard_map.145 = bf16[1024,512]{1,0:T(8,128)(2,1)S(1)} custom-call(bf16[1024,512]{1,0:T(8,128)(2,1)} %x_hbm.1, bf16[64,512]{1,0:T(8,128)(2,1)} %c1_hbm.1, bf16[4,512]{1,0:T(4,128)(2,1)} %c2_hbm.1, bf16[1,512]{1,0:T(2,128)(2,1)} %c3_hbm.1, s32[16,64]{1,0:T(8,128)} %bitcast.3, s32[16,64]{1,0:T(8,128)} %bitcast.4, s32[16,64]{1,0:T(8,128)} %bitcast.5, ...), custom_call_target="tpu_custom_call" | custom-call | tf_op jit(solution)/shard_map/pallas_call | solution.py:279
  23.3 1.0 %copy.17 = bf16[1024,512]{1,0:T(8,128)(2,1)} copy(bf16[1024,512]{1,0:T(8,128)(2,1)S(1)} %shard_map.145) | data formatting | bytes 2097152
